TPU v7x, 32 devices: a whole 2x2x4 slice. The times are simulated.
32 devices in a mesh: seq: 8 (over z, x), grp: 4 (over y, core).
Axes of the slice: x: 2, y: 2, z: 4, core: 2. Of those that a mesh axis runs over, the one named last changes fastest.
Arguments:
- query_proj: bfloat16 [2048, 4096], P('seq', 'grp'), may hold values from -6 to 6
- key_proj: bfloat16 [2048, 4096], P('seq', 'grp'), may hold values from -6 to 6
- value_proj: bfloat16 [2048, 4096], P('seq', 'grp'), may hold values from -6 to 6
- out_grad: bfloat16 [2048, 4096], P('seq', 'grp'), may hold values from -22 to 22
- filters: bfloat16 [256, 128], P('grp'), may hold values from -0.5 to 0.5
Outputs:
- query_grad: bfloat16 [2048, 4096], P('seq', 'grp')
- key_grad: bfloat16 [2048, 4096], P('seq', 'grp')
- value_grad: bfloat16 [2048, 4096], P('seq', 'grp')
- filter_grad: float32 [256, 128], P('grp')
All inputs are finite; a program needn't handle non-finite values.
Results may differ from a plain program's by a relative error of at most 0.005.
Values may be sent and summed in bfloat16 or wider, within the bound.
A program may use at most 64 MiB of HBM per device.

v0:
```python
import jax
import jax.numpy as jnp
from jax import lax
from jax.sharding import PartitionSpec as P

GSIZE = 16
K = 128
GROUPS = 256


def passed_along(value, axis, steps):
    count = lax.axis_size(axis)
    initial, last = (max(0, -steps), min(count, count - steps))
    return lax.ppermute(value, axis, [(source, source + steps) for source in range(initial, last)])


def forward_table(filt):
    group_n, tap_count = filt.shape
    return jnp.concatenate(
        [
            jnp.zeros((group_n, 1), filt.dtype),
            jnp.flip(filt, axis=1),
            jnp.zeros((group_n, 2 * tap_count - 1), filt.dtype),
        ],
        axis=1,
    )


def backward_table(filt):
    group_n, tap_count = filt.shape
    return jnp.concatenate([filt, jnp.zeros((group_n, 2 * tap_count), filt.dtype)], axis=1)


def toeplitz(table):
    group_n, span_all = table.shape
    tap_count = span_all // 3
    tiled_rows = jnp.tile(table, (1, tap_count))
    return tiled_rows[:, : tap_count * (span_all - 1)].reshape(group_n, tap_count, span_all - 1)[
        :, :, : 2 * tap_count
    ]


def diagonal_sums(matrix):
    group_n, tap_count, span_two = matrix.shape
    flat_rows = matrix.reshape(group_n, tap_count * span_two)
    padded = jnp.pad(flat_rows, ((0, 0), (0, tap_count)))
    skewed = padded.reshape(group_n, tap_count, span_two + 1)[:, :, 1 : tap_count + 1]
    return jnp.flip(jnp.sum(skewed, axis=1), axis=1)


def channel_major(rows, group_local):
    count = rows.shape[0]
    return rows.reshape(count, group_local, GSIZE).transpose(1, 2, 0)


def token_major(field):
    group_local, members, count = field.shape
    return field.transpose(2, 0, 1).reshape(count, group_local * members)


def paired_last(blocks):
    return jnp.concatenate([blocks[:, :, :-1], blocks[:, :, 1:]], axis=3)


def on_device(query_proj, key_proj, value_proj, out_grad, filters):
    rows_dev, chan_dev = query_proj.shape
    tap_count = filters.shape[1]
    group_local = filters.shape[0]
    block_count = rows_dev // tap_count
    edge_rows = tap_count - 1
    product_u = (key_proj.astype(jnp.float32) * value_proj.astype(jnp.float32)).astype(jnp.bfloat16)
    product_dz = (out_grad.astype(jnp.float32) * query_proj.astype(jnp.float32)).astype(
        jnp.bfloat16
    )
    key_tail, value_tail = passed_along(
        (key_proj[rows_dev - edge_rows :], value_proj[rows_dev - edge_rows :]), "seq", 1
    )
    earlier = (key_tail.astype(jnp.float32) * value_tail.astype(jnp.float32)).astype(jnp.bfloat16)
    grad_head, query_head = passed_along((out_grad[:edge_rows], query_proj[:edge_rows]), "seq", -1)
    later_rows = (grad_head.astype(jnp.float32) * query_head.astype(jnp.float32)).astype(
        jnp.bfloat16
    )
    zero_col = jnp.zeros((group_local, GSIZE, 1), jnp.bfloat16)
    extended_in = jnp.concatenate(
        [zero_col, channel_major(earlier, group_local), channel_major(product_u, group_local)],
        axis=2,
    ).reshape(group_local, GSIZE, block_count + 1, tap_count)
    extended_dz = jnp.concatenate(
        [channel_major(product_dz, group_local), channel_major(later_rows, group_local), zero_col],
        axis=2,
    ).reshape(group_local, GSIZE, block_count + 1, tap_count)
    forward_mat = toeplitz(forward_table(filters))
    backward_mat = toeplitz(backward_table(filters))
    pairs_in = paired_last(extended_in)
    conv_out = jnp.einsum(
        "gij,gcbj->gcbi", forward_mat, pairs_in, preferred_element_type=jnp.float32
    ).reshape(group_local, GSIZE, rows_dev)
    query_grad = (out_grad.astype(jnp.float32) * token_major(conv_out)).astype(jnp.bfloat16)
    grad_in = jnp.einsum(
        "gij,gcbj->gcbi", backward_mat, paired_last(extended_dz), preferred_element_type=jnp.float32
    ).reshape(group_local, GSIZE, rows_dev)
    grad_rows = token_major(grad_in)
    key_grad = (grad_rows * value_proj.astype(jnp.float32)).astype(jnp.bfloat16)
    value_grad = (grad_rows * key_proj.astype(jnp.float32)).astype(jnp.bfloat16)
    corr = jnp.einsum(
        "gcbi,gcbj->gij", extended_dz[:, :, :-1], pairs_in, preferred_element_type=jnp.float32
    )
    raw_local = diagonal_sums(corr)
    raw_sums = lax.psum(raw_local, "seq")
    squares = lax.psum(jnp.sum(raw_sums * raw_sums), "grp")
    factor = jnp.minimum(jnp.float32(1.0), jnp.sqrt(jnp.float32(GROUPS * K) / squares))
    filter_grad = raw_sums * factor
    return (query_grad, key_grad, value_grad, filter_grad)


def solution(mesh):
    return jax.shard_map(
        on_device,
        mesh=mesh,
        in_specs=(
            P("seq", "grp"),
            P("seq", "grp"),
            P("seq", "grp"),
            P("seq", "grp"),
            P("grp", None),
        ),
        out_specs=(P("seq", "grp"), P("seq", "grp"), P("seq", "grp"), P("grp", None)),
        check_vma=False,
    )
```

profile of v0, /device:TPU:0, one launch (start us, length us, event | category | flops | bytes accessed | tf_op | source)
XLA Modules:
  0.0 161.7 jit_solution(7608783810833465797)
XLA Ops:
  0.6 1.2 copy.9
  1.9 1.3 collective-permute-start.2
  3.2 1.2 copy.17
  5.2 1.3 collective-permute-start.3
  6.5 1.2 copy.10
  8.6 6.8 %collective-permute-start = (bf16[127,1024]{0,1:T(8,128)(2,1)}, bf16[127,1024]{0,1:T(8,128)(2,1)}, u32[]{:S(2)}, u32[]{:S(2)}) collective-permute-start(bf16[127,1024]{0,1:T(8,128)(2,1)} %slice.53), channel_id=1, source_target_pairs={{0,4},{4,8},{8,12},{12,16},{16,20},{20,24},{24,28},{1,5},{5,9},{9,... | collective-permute-start | bytes 780296 | tf_op jit(solution)/shard_map/ppermute | solution.py:14
  17.5 4.8 %collective-permute-start.1 = (bf16[127,1024]{0,1:T(8,128)(2,1)}, bf16[127,1024]{0,1:T(8,128)(2,1)}, u32[]{:S(2)}, u32[]{:S(2)}) collective-permute-start(bf16[127,1024]{0,1:T(8,128)(2,1)} %slice.54), channel_id=1, source_target_pairs={{0,4},{4,8},{8,12},{12,16},{16,20},{20,24},{24,28},{1,5},{5,9},{9,... | collective-permute-start | bytes 780296 | tf_op jit(solution)/shard_map/ppermute | solution.py:14
  23.0 4.1 %copy.36 = bf16[8,8,128,384]{3,1,2,0:T(8,128)(2,1)S(1)} copy(bf16[8,8,128,384]{3,2,1,0:T(8,128)(2,1)S(1)} %bitcast.58) | data formatting | bytes 12582912
  27.1 3.1 %slice.63 = bf16[64,49024]{1,0:T(8,128)(2,1)} slice(bf16[64,49152]{1,0:T(8,128)(2,1)S(1)} %bitcast.60), slice={[0:64], [0:49024]} | slice | bytes 12550144 | tf_op jit(solution)/shard_map/slice | solution.py:38
  30.2 16.4 %reshape.67 = bf16[64,128,383]{2,1,0:T(8,128)(2,1)} reshape(bf16[64,49024]{1,0:T(8,128)(2,1)} %slice.63) | data formatting | bytes 12550144 | tf_op jit(solution)/shard_map/reshape | solution.py:38
  47.3 4.1 %copy.35 = bf16[8,8,128,384]{3,1,2,0:T(8,128)(2,1)S(1)} copy(bf16[8,8,128,384]{3,2,1,0:T(8,128)(2,1)S(1)} %bitcast.59) | data formatting | bytes 12582912
  51.3 3.0 %slice.57 = bf16[64,49024]{1,0:T(8,128)(2,1)} slice(bf16[64,49152]{1,0:T(8,128)(2,1)S(1)} %bitcast.61), slice={[0:64], [0:49024]} | slice | bytes 12550144 | tf_op jit(solution)/shard_map/slice | solution.py:38
  54.4 16.5 %reshape.61 = bf16[64,128,383]{2,1,0:T(8,128)(2,1)} reshape(bf16[64,49024]{1,0:T(8,128)(2,1)} %slice.57) | data formatting | bytes 12550144 | tf_op jit(solution)/shard_map/reshape | solution.py:38
  72.2 2.6 %reshape.66 = bf16[64,16,3,128]{3,2,1,0:T(4,128)(2,1)S(1)} reshape(bf16[64,16,384]{2,1,0:T(8,128)(2,1)} %pad_maximum_fusion.1) | data formatting | bytes 1572864 | tf_op jit(solution)/shard_map/reshape | solution.py:91
  75.8 3.7 %fusion.3 = f32[64,2,2,8,128]{4,3,2,1,0:T(8,128)S(1)} fusion(bf16[64,128,383]{2,1,0:T(8,128)(2,1)} %reshape.67, bf16[64,16,2,128]{3,1,2,0:T(8,128)(2,1)S(1)} %copy.32, bf16[64,16,2,128]{3,1,2,0:T(8,128)(2,1)S(1)} %copy.31), kind=kOutput, calls=%fused_computation.6 | convolution fusion | flops 136314880 | bytes 6291456 | tf_op jit(solution)/shard_map/gij,gcbj->gcbi/dot_general | solution.py:99
  84.0 2.0 %copy.24 = bf16[256,1024]{1,0:T(8,128)(2,1)} copy(bf16[256,1024]{0,1:T(8,128)(2,1)} %get-tuple-element.9) | data formatting | bytes 1048576
  86.4 1.3 fusion.13
  89.0 1.5 fusion.2
  90.8 4.7 %copy.37 = f32[8,8,128,256]{3,1,2,0:T(8,128)S(1)} copy(f32[8,8,128,256]{3,2,1,0:T(8,128)S(1)} %bitcast.57) | data formatting | bytes 16777216
  95.5 3.7 %pad.5 = f32[64,32896]{1,0:T(8,128)} pad(f32[64,32768]{1,0:T(8,128)S(1)} %bitcast.56, f32[]{:T(128)} %constant.5.clone.1), padding=0_0x0_128 | pad | bytes 16809988 | tf_op jit(solution)/shard_map/jit(_pad)/pad | solution.py:46
  99.3 14.2 %reshape.71 = f32[64,128,257]{2,1,0:T(8,128)} reshape(f32[64,32896]{1,0:T(8,128)} %pad.5) | data formatting | bytes 16842752 | tf_op jit(solution)/shard_map/reshape | solution.py:47
  113.4 4.5 %slice_reduce_fusion = f32[64,128]{1,0:T(8,128)S(1)} fusion(f32[64,128,257]{2,1,0:T(8,128)} %reshape.71), kind=kLoop, calls=%fused_computation | loop fusion | flops 1040384 | bytes 4227072 | tf_op jit(solution)/shard_map/reduce_sum | solution.py:48
  118.1 34.4 %psum.14 = f32[64,128]{1,0:T(8,128)S(1)} all-reduce(f32[64,128]{1,0:T(8,128)S(1)} %rev.9), channel_id=1, replica_groups=mesh['seq'=8,'grp'=4] {'seq'}, use_global_device_ids=true, to_apply=%region_1.2 | all-reduce | flops 8192 | bytes 65536 | tf_op jit(solution)/shard_map/psum | solution.py:109
  154.1 6.3 %psum.15 = f32[]{:T(128)} all-reduce(f32[]{:T(128)} %multiply_reduce_fusion), channel_id=1, replica_groups=mesh['seq'=8,'grp'=4] {'grp'}, use_global_device_ids=true, to_apply=%region_3.4 | all-reduce | flops 1 | bytes 8 | tf_op jit(solution)/shard_map/psum | solution.py:110
  (46 shorter events, 15.9 us)
Async XLA Ops:
  0.6 21.7 %copy-start = (bf16[64,128]{1,0:T(8,128)(2,1)S(1)}, bf16[64,128]{1,0:T(8,128)(2,1)}, u32[]{:S(2)}) copy-start(bf16[64,128]{1,0:T(8,128)(2,1)} %param.9) | copy-start | bytes 49156
  1.9 69.1 %collective-permute-start.2 = (bf16[127,1024]{0,1:T(8,128)(2,1)S(1)}, bf16[127,1024]{0,1:T(8,128)(2,1)S(1)}, u32[]{:S(2)}, u32[]{:S(2)}) collective-permute-start(bf16[127,1024]{0,1:T(8,128)(2,1)S(1)} %slice.59), channel_id=1, source_target_pairs={{4,0},{8,4},{12,8},{16,12},{20,16},{24,20},{28,24},{5,1},{9,5},{13... | collective-permute-start | bytes 780296 | tf_op jit(solution)/shard_map/ppermute | solution.py:14
  5.2 65.8 %collective-permute-start.3 = (bf16[127,1024]{0,1:T(8,128)(2,1)}, bf16[127,1024]{0,1:T(8,128)(2,1)S(1)}, u32[]{:S(2)}, u32[]{:S(2)}) collective-permute-start(bf16[127,1024]{0,1:T(8,128)(2,1)} %slice.60), channel_id=1, source_target_pairs={{4,0},{8,4},{12,8},{16,12},{20,16},{24,20},{28,24},{5,1},{9,5},{13... | collective-permute-start | bytes 780296 | tf_op jit(solution)/shard_map/ppermute | solution.py:14
  8.6 73.1 %collective-permute-start = (bf16[127,1024]{0,1:T(8,128)(2,1)}, bf16[127,1024]{0,1:T(8,128)(2,1)}, u32[]{:S(2)}, u32[]{:S(2)}) collective-permute-start(bf16[127,1024]{0,1:T(8,128)(2,1)} %slice.53), channel_id=1, source_target_pairs={{0,4},{4,8},{8,12},{12,16},{16,20},{20,24},{24,28},{1,5},{5,9},{9,... | collective-permute-start | bytes 780296 | tf_op jit(solution)/shard_map/ppermute | solution.py:14
  17.5 64.2 %collective-permute-start.1 = (bf16[127,1024]{0,1:T(8,128)(2,1)}, bf16[127,1024]{0,1:T(8,128)(2,1)}, u32[]{:S(2)}, u32[]{:S(2)}) collective-permute-start(bf16[127,1024]{0,1:T(8,128)(2,1)} %slice.54), channel_id=1, source_target_pairs={{0,4},{4,8},{8,12},{12,16},{16,20},{20,24},{24,28},{1,5},{5,9},{9,... | collective-permute-start | bytes 780296 | tf_op jit(solution)/shard_map/ppermute | solution.py:14
  86.1 2.2 %slice-start = ((s8[6291456]{0:T(1024)(128)(4,1)}), s8[4194304]{0:T(1024)(128)(4,1)S(1)}, s32[]{:S(2)}) async-start(s8[6291456]{0:T(1024)(128)(4,1)} %bitcast.62), calls=%async_computation | async-start | bytes 8388608
  86.4 2.6 %slice-start.1 = ((s8[6291456]{0:T(1024)(128)(4,1)}), s8[2097152]{0:T(1024)(128)(4,1)S(1)}, s32[]{:S(2)}) async-start(s8[6291456]{0:T(1024)(128)(4,1)} %bitcast.62), calls=%async_computation.1 | async-start | bytes 4194304
where the time goes:
time: 163 us; the launch traced here: 162 us
  local copies, waits for them, and re-layouts  88.9 us (55%)
  blocking collectives  40.7 us (25%)
  starting transfers between devices  14.2 us (9%)
  other arithmetic  9.75 us (6%)
  matrix products  6.52 us (4%)
    psum x1, blocking collectives, on_device(): raw_sums = lax.psum(raw_local, 'seq')  34.4 us
    reshape x2, local copies, waits for them, and re-layouts, toeplitz(): tiled_rows[:, :tap_count * (span_all - 1)]  32.9 us
    unnamed x19, local copies, waits for them, and re-layouts  23.5 us
    ppermute x4, starting transfers between devices, passed_along(): lax.ppermute(value, axis, [(source, source + steps) for source in range(i...  14.2 us
    reshape x1, local copies, waits for them, and re-layouts, diagonal_sums(): padded.reshape(group_n, tap_count, span_two + 1)[:, :, 1:tap_count + 1]  14.2 us
    psum x1, blocking collectives, on_device(): squares = lax.psum(jnp.sum(raw_sums * raw_sums), 'grp')  6.27 us
    slice x2, local copies, waits for them, and re-layouts, toeplitz(): tiled_rows[:, :tap_count * (span_all - 1)]  6.14 us
    reduce_sum x1, other arithmetic, diagonal_sums(): return jnp.flip(jnp.sum(skewed, axis=1), axis=1)  4.53 us
  transfers between devices with their start and end apart: 4, of which 0 were waited for; matrix products, arithmetic and copies ran while one was open for 40% of the time, Pallas kernels for 0%

commit v1 on v0

v1 whole, which is shorter than its diff:
```python
import functools

import jax
import jax.numpy as jnp
from jax import lax
from jax.experimental import pallas as pl
from jax.experimental.pallas import tpu as pltpu
from jax.sharding import PartitionSpec as P

GSIZE = 16
LANES = 128
PER_TILE = LANES // GSIZE
MESH = pl.DeviceIdType.MESH
F32 = jnp.float32
BF16 = jnp.bfloat16


def product(a, b):
    return (a.astype(F32) * b.astype(F32)).astype(BF16)


def kernel(
    seq_n, grp_n, whole_sum, chunk_n,
    q_hbm, k_hbm, v_hbm, g_hbm, h_ref,
    qg_hbm, kg_hbm, vg_hbm, fg_ref,
    q, k, v, g, u, dz, u_halo, dz_halo, fmat, bmat, out_q, out_k, out_v,
    taps, raw, scattered, gathered, squares,
    in_sem, out_sem, halo_send, halo_recv, rs_send, rs_recv, ag_send, ag_recv, ss_send, ss_recv,
):
    me, mine = lax.axis_index("seq"), lax.axis_index("grp")
    tile_n = u.shape[0]
    half = LANES
    top, low = pl.ds(0, half), pl.ds(half, half)
    per_chunk = tile_n // chunk_n

    loads = []
    order = ((g_hbm, g, top), (q_hbm, q, top), (k_hbm, k, low), (v_hbm, v, low),
             (g_hbm, g, low), (q_hbm, q, low), (k_hbm, k, top), (v_hbm, v, top))
    for index, (source, target, rows) in enumerate(order):
        copy = pltpu.make_async_copy(source.at[rows], target.at[rows], in_sem.at[index])
        copy.start()
        loads.append(copy)

    def at_seq(position):
        return {"seq": position, "grp": mine}

    def at_grp(position):
        return {"seq": me, "grp": position}

    seq_peers = [lax.rem(me + step, seq_n) for step in range(1, seq_n)] if whole_sum else []
    grp_peers = [lax.rem(mine + step, grp_n) for step in range(1, grp_n)] if whole_sum else []
    has_left, has_right = me > 0, me < seq_n - 1
    barrier = pltpu.get_barrier_semaphore()
    if whole_sum:
        for peer in seq_peers:
            pl.semaphore_signal(barrier, 1, device_id=at_seq(peer), device_id_type=MESH)
        for peer in grp_peers:
            pl.semaphore_signal(barrier, 1, device_id=at_grp(peer), device_id_type=MESH)
    else:
        @pl.when(has_left)
        def _():
            pl.semaphore_signal(barrier, 1, device_id=at_seq(me - 1), device_id_type=MESH)

        @pl.when(has_right)
        def _():
            pl.semaphore_signal(barrier, 1, device_id=at_seq(me + 1), device_id_type=MESH)

    h = h_ref[...]
    row = lax.broadcasted_iota(jnp.int32, (half, half), 0)
    col = lax.broadcasted_iota(jnp.int32, (half, half), 1)
    flip = (((row + col) == 0) | ((row + col) == half)).astype(BF16)
    taps[0] = h.astype(F32)
    taps[1] = jnp.dot(h, flip, preferred_element_type=F32)

    @pl.when(jnp.logical_not(has_left))
    def _():
        u_halo[...] = jnp.zeros_like(u_halo)

    @pl.when(jnp.logical_not(has_right))
    def _():
        dz_halo[...] = jnp.zeros_like(dz_halo)

    def cols(tile):
        return pl.ds(pl.multiple_of(tile * LANES, LANES), LANES)

    def dz_copy(chunk):
        tiles = pl.ds(chunk * per_chunk, per_chunk)
        return pltpu.make_async_remote_copy(
            src_ref=dz.at[tiles, top], dst_ref=dz_halo.at[tiles],
            send_sem=halo_send.at[0, chunk], recv_sem=halo_recv.at[0, chunk],
            device_id=at_seq(me - 1), device_id_type=MESH)

    def u_copy(chunk):
        tiles = pl.ds(chunk * per_chunk, per_chunk)
        return pltpu.make_async_remote_copy(
            src_ref=u.at[tiles, low], dst_ref=u_halo.at[tiles],
            send_sem=halo_send.at[1, chunk], recv_sem=halo_recv.at[1, chunk],
            device_id=at_seq(me + 1), device_id_type=MESH)

    loads[0].wait()
    loads[1].wait()
    for tile in range(tile_n):
        dz[tile, top] = product(g[top, cols(tile)], q[top, cols(tile)])
    loads[2].wait()
    loads[3].wait()
    for tile in range(tile_n):
        u[tile, low] = product(k[low, cols(tile)], v[low, cols(tile)])

    if whole_sum:
        pl.semaphore_wait(barrier, seq_n + grp_n - 2)
    else:
        @pl.when(has_left)
        def _():
            pl.semaphore_wait(barrier, 1)

        @pl.when(has_right)
        def _():
            pl.semaphore_wait(barrier, 1)

    @pl.when(has_left)
    def _():
        for chunk in range(chunk_n):
            dz_copy(chunk).start()

    @pl.when(has_right)
    def _():
        for chunk in range(chunk_n):
            u_copy(chunk).start()

    for index in range(4, 8):
        loads[index].wait()
    for tile in range(tile_n):
        dz[tile, low] = product(g[low, cols(tile)], q[low, cols(tile)])
        u[tile, top] = product(k[top, cols(tile)], v[top, cols(tile)])

    lane_group = lax.broadcasted_iota(jnp.int32, (half, LANES), 1) // GSIZE

    def pick(stacked):
        out = stacked[0:half]
        for member in range(1, PER_TILE):
            out = jnp.where(lane_group == member, stacked[member * half:(member + 1) * half], out)
        return out

    def conv(table, tile, pair):
        return pick(jnp.dot(table[tile], pair, preferred_element_type=F32))

    def store_q(tile, rows, z):
        out_q[rows, cols(tile)] = (g[rows, cols(tile)].astype(F32) * z).astype(BF16)

    def store_kv(tile, rows, du):
        out_k[rows, cols(tile)] = (v[rows, cols(tile)].astype(F32) * du).astype(BF16)
        out_v[rows, cols(tile)] = (k[rows, cols(tile)].astype(F32) * du).astype(BF16)

    def local_part(tile, carry):
        base = pl.multiple_of(tile * PER_TILE, PER_TILE)
        plain = taps[0, pl.ds(base, PER_TILE), :]
        turned = taps[1, pl.ds(base, PER_TILE), :]
        for member in range(PER_TILE):
            rows = pl.ds(member * half, half)
            spread = jnp.broadcast_to(plain[member:member + 1], (half, half))
            circ = pltpu.roll(spread, 0, 1, stride=1, stride_axis=0)
            bmat[tile, rows, 0:half] = jnp.where(col >= row, circ, 0.0).astype(BF16)
            bmat[tile, rows, half:2 * half] = jnp.where(col < row, circ, 0.0).astype(BF16)
            spread = jnp.broadcast_to(turned[member:member + 1], (half, half))
            circ = pltpu.roll(spread, 0, 1, stride=1, stride_axis=0)
            fmat[tile, rows, 0:half] = jnp.where(col > row, circ, 0.0).astype(BF16)
            fmat[tile, rows, half:2 * half] = jnp.where(col <= row, circ, 0.0).astype(BF16)
        store_q(tile, low, conv(fmat, tile, u[tile]))
        store_kv(tile, top, conv(bmat, tile, dz[tile]))
        return carry

    lax.fori_loop(0, tile_n, local_part, 0)

    out_copies = []

    def send_out(source, target, rows):
        copy = pltpu.make_async_copy(source.at[rows], target.at[rows], out_sem.at[len(out_copies)])
        copy.start()
        out_copies.append(copy)

    send_out(out_q, qg_hbm, low)
    send_out(out_k, kg_hbm, top)
    send_out(out_v, vg_hbm, top)

    sub = lax.broadcasted_iota(jnp.int32, (PER_TILE, 8, LANES), 1)
    lanes256 = lax.broadcasted_iota(jnp.int32, (half, 2 * LANES), 1) % LANES // GSIZE

    def correlate(tile, carry):
        both = jnp.concatenate([u[tile, top], u[tile, low]], axis=1)
        window = jnp.concatenate(
            [jnp.concatenate([dz[tile, top], dz[tile, low]], axis=1),
             jnp.concatenate([dz[tile, low], dz_halo[tile]], axis=1)], axis=0)
        parts = []
        for member in range(PER_TILE):
            left = jnp.where(lanes256 == member, both, jnp.zeros_like(both))
            c = lax.dot_general(left, window, (((1,), (1,)), ((), ())), preferred_element_type=F32)
            m = jnp.where(col >= row, c[:, :half], c[:, half:])
            size = half // 2
            while size >= 8:
                m = m[:size] + pltpu.roll(m[size:], LANES - size, 1)
                size //= 2
            parts.append(m.reshape(1, 8, LANES))
        folded = jnp.concatenate(parts, axis=0)
        for bit in (1, 2, 4):
            folded = jnp.where((sub & bit) != 0, pltpu.roll(folded, LANES - bit, 2), folded)
        raw[pl.ds(pl.multiple_of(tile * PER_TILE, PER_TILE), PER_TILE), :] = jnp.sum(folded, axis=1)
        return carry

    for chunk in range(chunk_n):
        @pl.when(has_right)
        def _():
            dz_copy(chunk).wait_recv()

        lax.fori_loop(chunk * per_chunk, (chunk + 1) * per_chunk, correlate, 0)

    if whole_sum:
        own = raw.shape[0] // seq_n
        my_rows = pl.ds(pl.multiple_of(me * own, own), own)
        rs_copies, ag_copies, ss_copies = [], [], []
        for step, peer in enumerate(seq_peers):
            rs_copies.append(pltpu.make_async_remote_copy(
                src_ref=raw.at[pl.ds(pl.multiple_of(peer * own, own), own)],
                dst_ref=scattered.at[step], send_sem=rs_send.at[step], recv_sem=rs_recv.at[step],
                device_id=at_seq(peer), device_id_type=MESH))
            rs_copies[-1].start()
    else:
        fg_ref[...] = raw[...]

    def halo_q(tile, carry):
        pair = jnp.concatenate([u_halo[tile], u[tile, top]], axis=0)
        store_q(tile, top, conv(fmat, tile, pair))
        return carry

    def halo_kv(tile, carry):
        pair = jnp.concatenate([dz[tile, low], dz_halo[tile]], axis=0)
        store_kv(tile, low, conv(bmat, tile, pair))
        return carry

    lax.fori_loop(0, tile_n, halo_kv, 0)
    send_out(out_k, kg_hbm, low)
    send_out(out_v, vg_hbm, low)

    if whole_sum:
        total = raw[my_rows]
        for step, copy in enumerate(rs_copies):
            copy.wait_recv()
            total = total + scattered[step]
        gathered[my_rows] = total
        for step, peer in enumerate(seq_peers):
            ag_copies.append(pltpu.make_async_remote_copy(
                src_ref=gathered.at[my_rows], dst_ref=gathered.at[my_rows],
                send_sem=ag_send.at[step], recv_sem=ag_recv.at[step],
                device_id=at_seq(peer), device_id_type=MESH))
            ag_copies[-1].start()

    first = max(1, chunk_n // 2)
    for chunk in range(first):
        @pl.when(has_left)
        def _():
            u_copy(chunk).wait_recv()

    lax.fori_loop(0, first * per_chunk, halo_q, 0)

    if whole_sum:
        for copy in ag_copies:
            copy.wait_recv()
        values = gathered[...]
        part = jnp.sum((values * values).reshape(-1, 8, LANES), axis=0)
        squares[0] = part
        for step, peer in enumerate(grp_peers):
            ss_copies.append(pltpu.make_async_remote_copy(
                src_ref=squares.at[0], dst_ref=squares.at[step + 1],
                send_sem=ss_send.at[step], recv_sem=ss_recv.at[step],
                device_id=at_grp(peer), device_id_type=MESH))
            ss_copies[-1].start()

    for chunk in range(first, chunk_n):
        @pl.when(has_left)
        def _():
            u_copy(chunk).wait_recv()

    lax.fori_loop(first * per_chunk, tile_n, halo_q, 0)
    send_out(out_q, qg_hbm, top)

    if whole_sum:
        for copy in ss_copies:
            copy.wait_recv()
        ss = jnp.sum(jnp.sum(squares[...], axis=0), keepdims=True)
        count = F32(raw.shape[0] * grp_n * LANES)
        factor = jnp.minimum(F32(1.0), jnp.sqrt(count / ss))
        fg_ref[...] = gathered[...] * factor
        for copy in rs_copies + ag_copies + ss_copies:
            copy.wait_send()

    @pl.when(has_left)
    def _():
        for chunk in range(chunk_n):
            dz_copy(chunk).wait_send()

    @pl.when(has_right)
    def _():
        for chunk in range(chunk_n):
            u_copy(chunk).wait_send()

    for copy in out_copies:
        copy.wait()


def on_device(seq_n, grp_n, query_proj, key_proj, value_proj, out_grad, filters):
    rows, chan = query_proj.shape
    group_n, tap_n = filters.shape
    assert tap_n == LANES and rows == 2 * LANES and chan == group_n * GSIZE
    tile_n = chan // LANES
    chunk_n = 4 if tile_n % 4 == 0 else 1
    whole_sum = group_n % (8 * seq_n) == 0
    own = group_n // seq_n if whole_sum else 8
    dense = jax.ShapeDtypeStruct((rows, chan), BF16)
    anywhere = pl.BlockSpec(memory_space=pl.ANY)
    vmem = pl.BlockSpec(memory_space=pltpu.VMEM)
    flat = pltpu.VMEM((rows, chan), BF16)
    dma = pltpu.SemaphoreType.DMA
    query_grad, key_grad, value_grad, sums = pl.pallas_call(
        functools.partial(kernel, seq_n, grp_n, whole_sum, chunk_n),
        out_shape=(dense, dense, dense, jax.ShapeDtypeStruct((group_n, tap_n), F32)),
        in_specs=[anywhere] * 4 + [vmem],
        out_specs=(anywhere, anywhere, anywhere, vmem),
        scratch_shapes=[flat] * 4
        + [pltpu.VMEM((tile_n, rows, LANES), BF16)] * 2
        + [pltpu.VMEM((tile_n, LANES, LANES), BF16)] * 2
        + [pltpu.VMEM((tile_n, PER_TILE * LANES, 2 * LANES), BF16)] * 2
        + [flat] * 3
        + [
            pltpu.VMEM((2, group_n, LANES), F32),
            pltpu.VMEM((group_n, LANES), F32),
            pltpu.VMEM((seq_n, own, LANES), F32),
            pltpu.VMEM((group_n, LANES), F32),
            pltpu.VMEM((grp_n, 8, LANES), F32),
            dma((8,)), dma((6,)), dma((2, chunk_n)), dma((2, chunk_n)),
            dma((seq_n,)), dma((seq_n,)), dma((seq_n,)), dma((seq_n,)),
            dma((grp_n,)), dma((grp_n,)),
        ],
        compiler_params=pltpu.CompilerParams(
            collective_id=0, has_side_effects=True, vmem_limit_bytes=48 * 1024 * 1024
        ),
        cost_estimate=pl.CostEstimate(
            flops=12 * rows * chan * LANES * PER_TILE, bytes_accessed=14 * rows * chan, transcendentals=0
        ),
    )(query_proj, key_proj, value_proj, out_grad, filters)
    if whole_sum:
        return query_grad, key_grad, value_grad, sums
    sums = lax.psum(sums, "seq")
    squares = lax.psum(jnp.sum(sums * sums), "grp")
    factor = jnp.minimum(F32(1.0), jnp.sqrt(F32(group_n * grp_n * tap_n) / squares))
    return query_grad, key_grad, value_grad, sums * factor


def solution(mesh):
    split = P("seq", "grp")
    return jax.shard_map(
        functools.partial(on_device, mesh.shape["seq"], mesh.shape["grp"]),
        mesh=mesh,
        in_specs=(split, split, split, split, P("grp", None)),
        out_specs=(split, split, split, P("grp", None)),
        check_vma=False,
    )
```

time: 163 us -> 42.9 us (0.26)
  local copies, waits for them, and re-layouts: 88.9 us -> 7.87 us
  blocking collectives: 40.7 us -> 0 us
  Pallas kernels: 0 us -> 34 us
  starting transfers between devices: 14.2 us -> 0 us
  other arithmetic: 9.75 us -> 0 us
  matrix products: 6.52 us -> 0 us
    reshape x7 -> x0, local copies, waits for them, and re-layouts: 50.1 us -> none  [the longest x2 32.9 us: toeplitz(): tiled_rows[:, :tap_count * (span_all - 1)]]
    psum x2 -> x0, blocking collectives: 40.7 us -> none  [the longest x1 34.4 us: on_device(): raw_sums = lax.psum(raw_local, 'seq')]
    pallas_call x0 -> x1, Pallas kernels: none -> 34 us  [on_device(): pl.pallas_call(functools.partial(kernel, seq_n, grp_n, whole_sum, chunk_n...]
    unnamed x19 -> x14, local copies, waits for them, and re-layouts: 23.5 us -> 7.87 us
    ppermute x4 -> x0, starting transfers between devices: 14.2 us -> none  [passed_along(): lax.ppermute(value, axis, [(source, source + steps) for source in range(i...]
    slice x8 -> x0, local copies, waits for them, and re-layouts: 10 us -> none  [the longest x2 6.14 us: toeplitz(): tiled_rows[:, :tap_count * (span_all - 1)]]
    dot_general x3 -> x0, matrix products: 6.52 us -> none  [the longest x1 3.71 us: on_device(): jnp.einsum('gij,gcbj->gcbi', backward_mat, paired_last(extended_dz), pref...]
    reduce_sum x2 -> x0, other arithmetic: 5.14 us -> none  [the longest x1 4.53 us: diagonal_sums(): return jnp.flip(jnp.sum(skewed, axis=1), axis=1)]
  transfers between devices with their start and end apart: 4 -> 0, of which waited for: 0 -> 0; matrix products, arithmetic and copies ran while one was open for 40% -> 0% of each run, Pallas kernels for 0% -> 0%
where the time goes in v1:
time: 42.9 us; the launch traced here: 42.6 us
  Pallas kernels  34 us (79%)
  local copies, waits for them, and re-layouts  7.87 us (18%)
  between operations  0.65 us (2%)
    pallas_call x1, Pallas kernels, on_device(): pl.pallas_call(functools.partial(kernel, seq_n, grp_n, whole_sum, chunk_n...  34 us
    unnamed x14, local copies, waits for them, and re-layouts  7.87 us

profile of v1, /device:TPU:0, one launch (start us, length us, event | category | flops | bytes accessed | tf_op | source)
XLA Modules:
  0.0 42.6 jit_solution(1035092631445450005)
XLA Ops:
  0.6 0.0 copy-start
  0.6 1.0 %copy-done = bf16[256,1024]{1,0:T(8,128)(2,1)S(1)} copy-done((bf16[256,1024]{1,0:T(8,128)(2,1)S(1)}, bf16[256,1024]{1,0:T(8,128)(2,1)}, u32[]{:S(2)}) %copy-start) | copy-done | bytes 524312
  1.7 0.0 copy-start.1
  1.7 1.0 %copy-done.1 = bf16[256,1024]{1,0:T(8,128)(2,1)S(1)} copy-done((bf16[256,1024]{1,0:T(8,128)(2,1)S(1)}, bf16[256,1024]{1,0:T(8,128)(2,1)}, u32[]{:S(2)}) %copy-start.1) | copy-done | bytes 524312
  2.7 0.0 copy-start.2
  2.7 1.0 %copy-done.2 = bf16[256,1024]{1,0:T(8,128)(2,1)S(1)} copy-done((bf16[256,1024]{1,0:T(8,128)(2,1)S(1)}, bf16[256,1024]{1,0:T(8,128)(2,1)}, u32[]{:S(2)}) %copy-start.2) | copy-done | bytes 524312
  3.8 0.0 copy-start.3
  3.8 1.0 %copy-done.3 = bf16[256,1024]{1,0:T(8,128)(2,1)S(1)} copy-done((bf16[256,1024]{1,0:T(8,128)(2,1)S(1)}, bf16[256,1024]{1,0:T(8,128)(2,1)}, u32[]{:S(2)}) %copy-start.3) | copy-done | bytes 524312
  4.8 0.0 copy-start.4
  4.8 0.7 %copy-done.4 = bf16[64,128]{1,0:T(8,128)(2,1)S(1)} copy-done((bf16[64,128]{1,0:T(8,128)(2,1)S(1)}, bf16[64,128]{1,0:T(8,128)(2,1)}, u32[]{:S(2)}) %copy-start.4) | copy-done | bytes 16408
  5.5 34.0 %shard_map.84 = (bf16[256,1024]{1,0:T(8,128)(2,1)S(1)}, bf16[256,1024]{1,0:T(8,128)(2,1)S(1)}, bf16[256,1024]{1,0:T(8,128)(2,1)S(1)}, f32[64,128]{1,0:T(8,128)S(1)}) custom-call(bf16[256,1024]{1,0:T(8,128)(2,1)S(1)} %copy-done, bf16[256,1024]{1,0:T(8,128)(2,1)S(1)} %copy-done.1, bf16[256,1024]{1,0:T(8,128)(2,1)S(1)} %copy-done.2, ...), custom_call_target="tpu_custom_call" | custom-call | flops 3221225472 | bytes 3670016 | tf_op jit(solution)/shard_map/pallas_call | solution.py:322
  39.6 0.8 %copy.13 = bf16[256,1024]{1,0:T(8,128)(2,1)} copy(bf16[256,1024]{1,0:T(8,128)(2,1)S(1)} %get-tuple-element.8) | data formatting | bytes 1048576
  40.4 0.8 %copy.14 = bf16[256,1024]{1,0:T(8,128)(2,1)} copy(bf16[256,1024]{1,0:T(8,128)(2,1)S(1)} %get-tuple-element.9) | data formatting | bytes 1048576
  41.2 0.8 %copy.15 = bf16[256,1024]{1,0:T(8,128)(2,1)} copy(bf16[256,1024]{1,0:T(8,128)(2,1)S(1)} %get-tuple-element.10) | data formatting | bytes 1048576
  42.0 0.6 %copy.16 = f32[64,128]{1,0:T(8,128)} copy(f32[64,128]{1,0:T(8,128)S(1)} %get-tuple-element.11) | data formatting | bytes 65536
Async XLA Ops:
  0.6 1.0 %copy-start = (bf16[256,1024]{1,0:T(8,128)(2,1)S(1)}, bf16[256,1024]{1,0:T(8,128)(2,1)}, u32[]{:S(2)}) copy-start(bf16[256,1024]{1,0:T(8,128)(2,1)} %q_hbm.1) | copy-start | bytes 1572868
  1.7 1.0 %copy-start.1 = (bf16[256,1024]{1,0:T(8,128)(2,1)S(1)}, bf16[256,1024]{1,0:T(8,128)(2,1)}, u32[]{:S(2)}) copy-start(bf16[256,1024]{1,0:T(8,128)(2,1)} %k_hbm.1) | copy-start | bytes 1572868
  2.7 1.0 %copy-start.2 = (bf16[256,1024]{1,0:T(8,128)(2,1)S(1)}, bf16[256,1024]{1,0:T(8,128)(2,1)}, u32[]{:S(2)}) copy-start(bf16[256,1024]{1,0:T(8,128)(2,1)} %v_hbm.1) | copy-start | bytes 1572868
  3.8 1.0 %copy-start.3 = (bf16[256,1024]{1,0:T(8,128)(2,1)S(1)}, bf16[256,1024]{1,0:T(8,128)(2,1)}, u32[]{:S(2)}) copy-start(bf16[256,1024]{1,0:T(8,128)(2,1)} %g_hbm.1) | copy-start | bytes 1572868
  4.8 0.7 %copy-start.4 = (bf16[64,128]{1,0:T(8,128)(2,1)S(1)}, bf16[64,128]{1,0:T(8,128)(2,1)}, u32[]{:S(2)}) copy-start(bf16[64,128]{1,0:T(8,128)(2,1)} %h_ref.1) | copy-start | bytes 49156

commit v2 on v1

--- a/solution.py
+++ b/solution.py
@@ -10,6 +10,8 @@
 GSIZE = 16
 LANES = 128
 PER_TILE = LANES // GSIZE
+CORR_BATCH = 8
+UNROLL = 2
 MESH = pl.DeviceIdType.MESH
 F32 = jnp.float32
 BF16 = jnp.bfloat16
@@ -121,11 +123,6 @@
     def _():
         for chunk in range(chunk_n):
             dz_copy(chunk).start()
-
-    @pl.when(has_right)
-    def _():
-        for chunk in range(chunk_n):
-            u_copy(chunk).start()
 
     for index in range(4, 8):
         loads[index].wait()
@@ -169,7 +166,16 @@
         store_kv(tile, top, conv(bmat, tile, dz[tile]))
         return carry
 
-    lax.fori_loop(0, tile_n, local_part, 0)
+    early = max(1, tile_n // 2)
+    lax.fori_loop(0, early, local_part, 0, unroll=UNROLL)
+
+    @pl.when(has_left)
+    def _():
+        for chunk in range(chunk_n):
+            dz_copy(chunk).wait_send()
+
+
+    lax.fori_loop(early, tile_n, local_part, 0, unroll=UNROLL)
 
     out_copies = []
 
@@ -191,15 +197,19 @@
             [jnp.concatenate([dz[tile, top], dz[tile, low]], axis=1),
              jnp.concatenate([dz[tile, low], dz_halo[tile]], axis=1)], axis=0)
         parts = []
-        for member in range(PER_TILE):
-            left = jnp.where(lanes256 == member, both, jnp.zeros_like(both))
+        for start in range(0, PER_TILE, CORR_BATCH):
+            members = range(start, start + CORR_BATCH)
+            left = jnp.concatenate(
+                [jnp.where(lanes256 == member, both, jnp.zeros_like(both)) for member in members], axis=0)
             c = lax.dot_general(left, window, (((1,), (1,)), ((), ())), preferred_element_type=F32)
-            m = jnp.where(col >= row, c[:, :half], c[:, half:])
-            size = half // 2
-            while size >= 8:
-                m = m[:size] + pltpu.roll(m[size:], LANES - size, 1)
-                size //= 2
-            parts.append(m.reshape(1, 8, LANES))
+            for place in range(CORR_BATCH):
+                rows = slice(place * half, (place + 1) * half)
+                m = jnp.where(col >= row, c[rows, :half], c[rows, half:])
+                size = half // 2
+                while size >= 8:
+                    m = m[:size] + pltpu.roll(m[size:], LANES - size, 1)
+                    size //= 2
+                parts.append(m.reshape(1, 8, LANES))
         folded = jnp.concatenate(parts, axis=0)
         for bit in (1, 2, 4):
             folded = jnp.where((sub & bit) != 0, pltpu.roll(folded, LANES - bit, 2), folded)
@@ -211,7 +221,7 @@
         def _():
             dz_copy(chunk).wait_recv()
 
-        lax.fori_loop(chunk * per_chunk, (chunk + 1) * per_chunk, correlate, 0)
+        lax.fori_loop(chunk * per_chunk, (chunk + 1) * per_chunk, correlate, 0, unroll=UNROLL)
 
     if whole_sum:
         own = raw.shape[0] // seq_n
@@ -226,6 +236,11 @@
     else:
         fg_ref[...] = raw[...]
 
+    @pl.when(has_right)
+    def _():
+        for chunk in range(chunk_n):
+            u_copy(chunk).start()
+
     def halo_q(tile, carry):
         pair = jnp.concatenate([u_halo[tile], u[tile, top]], axis=0)
         store_q(tile, top, conv(fmat, tile, pair))
@@ -236,7 +251,7 @@
         store_kv(tile, low, conv(bmat, tile, pair))
         return carry
 
-    lax.fori_loop(0, tile_n, halo_kv, 0)
+    lax.fori_loop(0, tile_n, halo_kv, 0, unroll=UNROLL)
     send_out(out_k, kg_hbm, low)
     send_out(out_v, vg_hbm, low)
 
@@ -259,7 +274,7 @@
         def _():
             u_copy(chunk).wait_recv()
 
-    lax.fori_loop(0, first * per_chunk, halo_q, 0)
+    lax.fori_loop(0, first * per_chunk, halo_q, 0, unroll=UNROLL)
 
     if whole_sum:
         for copy in ag_copies:
@@ -279,7 +294,7 @@
         def _():
             u_copy(chunk).wait_recv()
 
-    lax.fori_loop(first * per_chunk, tile_n, halo_q, 0)
+    lax.fori_loop(first * per_chunk, tile_n, halo_q, 0, unroll=UNROLL)
     send_out(out_q, qg_hbm, top)
 
     if whole_sum:
@@ -291,11 +306,6 @@
         fg_ref[...] = gathered[...] * factor
         for copy in rs_copies + ag_copies + ss_copies:
             copy.wait_send()
-
-    @pl.when(has_left)
-    def _():
-        for chunk in range(chunk_n):
-            dz_copy(chunk).wait_send()
 
     @pl.when(has_right)
     def _():
@@ -340,7 +350,7 @@
             dma((grp_n,)), dma((grp_n,)),
         ],
         compiler_params=pltpu.CompilerParams(
-            collective_id=0, has_side_effects=True, vmem_limit_bytes=48 * 1024 * 1024
+            collective_id=0, has_side_effects=True, vmem_limit_bytes=60 * 1024 * 1024
         ),
         cost_estimate=pl.CostEstimate(
             flops=12 * rows * chan * LANES * PER_TILE, bytes_accessed=14 * rows * chan, transcendentals=0

time: 42.9 us -> 35.5 us (0.83)
  Pallas kernels: 34 us -> 30 us
  local copies, waits for them, and re-layouts: 7.87 us -> 4.57 us
    pallas_call x1, Pallas kernels: 34 us -> 30 us  [on_device(): pl.pallas_call(functools.partial(kernel, seq_n, grp_n, whole_sum, chunk_n...]
    unnamed x14 -> x10, local copies, waits for them, and re-layouts: 7.87 us -> 4.57 us
where the time goes in v2:
time: 35.5 us; the launch traced here: 35.2 us
  Pallas kernels  30 us (85%)
  local copies, waits for them, and re-layouts  4.57 us (13%)
  between operations  0.65 us (2%)
    pallas_call x1, Pallas kernels, on_device(): pl.pallas_call(functools.partial(kernel, seq_n, grp_n, whole_sum, chunk_n...  30 us
    unnamed x10, local copies, waits for them, and re-layouts  4.57 us

profile of v2, /device:TPU:0, one launch (start us, length us, event | category | flops | bytes accessed | tf_op | source)
XLA Modules:
  0.0 35.2 jit_solution(18350979748443673154)
XLA Ops:
  0.6 30.0 %shard_map.84 = (bf16[256,1024]{1,0:T(8,128)(2,1)}, bf16[256,1024]{1,0:T(8,128)(2,1)}, bf16[256,1024]{1,0:T(8,128)(2,1)}, f32[64,128]{1,0:T(8,128)}) custom-call(bf16[256,1024]{1,0:T(8,128)(2,1)} %q_hbm.1, bf16[256,1024]{1,0:T(8,128)(2,1)} %k_hbm.1, bf16[256,1024]{1,0:T(8,128)(2,1)} %v_hbm.1, bf16[256,1024]{1,0:T(8,128)(2,1)} %g_hbm.1, bf16[64,128]{1,0:T(8,128)(2,1)} %h_ref.1), custom_call_target="tpu_custom_call" | custom-call | flops 3221225472 | bytes 3670016 | tf_op jit(solution)/shard_map/pallas_call | solution.py:332
  30.6 0.0 copy-start.1
  30.6 1.9 %copy.13 = bf16[256,1024]{1,0:T(8,128)(2,1)} copy(bf16[256,1024]{1,0:T(8,128)(2,1)} %get-tuple-element.8) | data formatting | bytes 1048576
  32.5 0.0 copy-done.1
  32.5 0.0 copy-start
  32.5 0.8 %copy.14 = bf16[256,1024]{1,0:T(8,128)(2,1)} copy(bf16[256,1024]{1,0:T(8,128)(2,1)S(1)} %copy-done.1) | data formatting | bytes 1048576
  33.3 0.4 %copy-done = bf16[256,1024]{1,0:T(8,128)(2,1)S(1)} copy-done((bf16[256,1024]{1,0:T(8,128)(2,1)S(1)}, bf16[256,1024]{1,0:T(8,128)(2,1)}, u32[]{:S(2)}) %copy-start) | copy-done | bytes 524312
  33.8 0.0 copy-start.2
  33.8 0.8 %copy.15 = bf16[256,1024]{1,0:T(8,128)(2,1)} copy(bf16[256,1024]{1,0:T(8,128)(2,1)S(1)} %copy-done) | data formatting | bytes 1048576
  34.6 0.0 copy-done.2
  34.6 0.6 %copy.16 = f32[64,128]{1,0:T(8,128)} copy(f32[64,128]{1,0:T(8,128)S(1)} %copy-done.2) | data formatting | bytes 65536
Async XLA Ops:
  30.6 1.9 %copy-start.1 = (bf16[256,1024]{1,0:T(8,128)(2,1)S(1)}, bf16[256,1024]{1,0:T(8,128)(2,1)}, u32[]{:S(2)}) copy-start(bf16[256,1024]{1,0:T(8,128)(2,1)} %get-tuple-element.9) | copy-start | bytes 1572868
  32.5 1.2 %copy-start = (bf16[256,1024]{1,0:T(8,128)(2,1)S(1)}, bf16[256,1024]{1,0:T(8,128)(2,1)}, u32[]{:S(2)}) copy-start(bf16[256,1024]{1,0:T(8,128)(2,1)} %get-tuple-element.10) | copy-start | bytes 1572868
  33.8 0.8 %copy-start.2 = (f32[64,128]{1,0:T(8,128)S(1)}, f32[64,128]{1,0:T(8,128)}, u32[]{:S(2)}) copy-start(f32[64,128]{1,0:T(8,128)} %get-tuple-element.11) | copy-start | bytes 98308

commit v3 on v2

--- a/solution.py
+++ b/solution.py
@@ -23,10 +23,10 @@
 
 def kernel(
     seq_n, grp_n, whole_sum, chunk_n,
-    q_hbm, k_hbm, v_hbm, g_hbm, h_ref,
+    q_hbm, k_hbm, v_hbm, g_hbm, h_hbm,
     qg_hbm, kg_hbm, vg_hbm, fg_ref,
-    q, k, v, g, u, dz, u_halo, dz_halo, fmat, bmat, out_q, out_k, out_v,
-    taps, raw, scattered, gathered, squares,
+    q, k, v, g, h_own, u, dz, u_halo, dz_halo, fmat, bmat, out_q, out_k, out_v,
+    taps, raw, scattered, gathered, squares, own_square,
     in_sem, out_sem, halo_send, halo_recv, rs_send, rs_recv, ag_send, ag_recv, ss_send, ss_recv,
 ):
     me, mine = lax.axis_index("seq"), lax.axis_index("grp")
@@ -42,22 +42,27 @@
         copy = pltpu.make_async_copy(source.at[rows], target.at[rows], in_sem.at[index])
         copy.start()
         loads.append(copy)
+    load_h = pltpu.make_async_copy(h_hbm, h_own, in_sem.at[len(order)])
+    load_h.start()
 
     def at_seq(position):
         return {"seq": position, "grp": mine}
 
-    def at_grp(position):
-        return {"seq": me, "grp": position}
+    def at(seq_at, grp_at):
+        return {"seq": seq_at, "grp": grp_at}
 
     seq_peers = [lax.rem(me + step, seq_n) for step in range(1, seq_n)] if whole_sum else []
-    grp_peers = [lax.rem(mine + step, grp_n) for step in range(1, grp_n)] if whole_sum else []
+    far_peers = [
+        (lax.rem(me + seq_step, seq_n), lax.rem(mine + grp_step, grp_n))
+        for grp_step in range(1, grp_n) for seq_step in range(seq_n)
+    ] if whole_sum else []
     has_left, has_right = me > 0, me < seq_n - 1
     barrier = pltpu.get_barrier_semaphore()
     if whole_sum:
         for peer in seq_peers:
             pl.semaphore_signal(barrier, 1, device_id=at_seq(peer), device_id_type=MESH)
-        for peer in grp_peers:
-            pl.semaphore_signal(barrier, 1, device_id=at_grp(peer), device_id_type=MESH)
+        for peer in far_peers:
+            pl.semaphore_signal(barrier, 1, device_id=at(*peer), device_id_type=MESH)
     else:
         @pl.when(has_left)
         def _():
@@ -66,13 +71,6 @@
         @pl.when(has_right)
         def _():
             pl.semaphore_signal(barrier, 1, device_id=at_seq(me + 1), device_id_type=MESH)
-
-    h = h_ref[...]
-    row = lax.broadcasted_iota(jnp.int32, (half, half), 0)
-    col = lax.broadcasted_iota(jnp.int32, (half, half), 1)
-    flip = (((row + col) == 0) | ((row + col) == half)).astype(BF16)
-    taps[0] = h.astype(F32)
-    taps[1] = jnp.dot(h, flip, preferred_element_type=F32)
 
     @pl.when(jnp.logical_not(has_left))
     def _():
@@ -103,32 +101,40 @@
     loads[1].wait()
     for tile in range(tile_n):
         dz[tile, top] = product(g[top, cols(tile)], q[top, cols(tile)])
+    if whole_sum:
+        pl.semaphore_wait(barrier, seq_n * grp_n - 1)
+    else:
+        @pl.when(has_left)
+        def _():
+            pl.semaphore_wait(barrier, 1)
+
+        @pl.when(has_right)
+        def _():
+            pl.semaphore_wait(barrier, 1)
+
+    @pl.when(has_left)
+    def _():
+        for chunk in range(chunk_n):
+            dz_copy(chunk).start()
+
     loads[2].wait()
     loads[3].wait()
     for tile in range(tile_n):
         u[tile, low] = product(k[low, cols(tile)], v[low, cols(tile)])
-
-    if whole_sum:
-        pl.semaphore_wait(barrier, seq_n + grp_n - 2)
-    else:
-        @pl.when(has_left)
-        def _():
-            pl.semaphore_wait(barrier, 1)
-
-        @pl.when(has_right)
-        def _():
-            pl.semaphore_wait(barrier, 1)
-
-    @pl.when(has_left)
-    def _():
-        for chunk in range(chunk_n):
-            dz_copy(chunk).start()
 
     for index in range(4, 8):
         loads[index].wait()
     for tile in range(tile_n):
         dz[tile, low] = product(g[low, cols(tile)], q[low, cols(tile)])
         u[tile, top] = product(k[top, cols(tile)], v[top, cols(tile)])
+
+    load_h.wait()
+    h = h_own[...]
+    row = lax.broadcasted_iota(jnp.int32, (half, half), 0)
+    col = lax.broadcasted_iota(jnp.int32, (half, half), 1)
+    flip = (((row + col) == 0) | ((row + col) == half)).astype(BF16)
+    taps[0] = h.astype(F32)
+    taps[1] = jnp.dot(h, flip, preferred_element_type=F32)
 
     lane_group = lax.broadcasted_iota(jnp.int32, (half, LANES), 1) // GSIZE
 
@@ -261,49 +267,39 @@
             copy.wait_recv()
             total = total + scattered[step]
         gathered[my_rows] = total
+        own_square[...] = jnp.sum(total * total, axis=0, keepdims=True)
         for step, peer in enumerate(seq_peers):
             ag_copies.append(pltpu.make_async_remote_copy(
                 src_ref=gathered.at[my_rows], dst_ref=gathered.at[my_rows],
                 send_sem=ag_send.at[step], recv_sem=ag_recv.at[step],
                 device_id=at_seq(peer), device_id_type=MESH))
             ag_copies[-1].start()
-
-    first = max(1, chunk_n // 2)
-    for chunk in range(first):
+        for slot, peer in enumerate(far_peers):
+            ss_copies.append(pltpu.make_async_remote_copy(
+                src_ref=own_square, dst_ref=squares.at[pl.ds(slot, 1)],
+                send_sem=ss_send.at[slot], recv_sem=ss_recv.at[slot],
+                device_id=at(*peer), device_id_type=MESH))
+            ss_copies[-1].start()
+
+    for chunk in range(chunk_n):
         @pl.when(has_left)
         def _():
             u_copy(chunk).wait_recv()
 
-    lax.fori_loop(0, first * per_chunk, halo_q, 0, unroll=UNROLL)
-
-    if whole_sum:
-        for copy in ag_copies:
+        lax.fori_loop(chunk * per_chunk, (chunk + 1) * per_chunk, halo_q, 0, unroll=UNROLL)
+
+    send_out(out_q, qg_hbm, top)
+
+    if whole_sum:
+        for copy in ag_copies + ss_copies:
             copy.wait_recv()
         values = gathered[...]
-        part = jnp.sum((values * values).reshape(-1, 8, LANES), axis=0)
-        squares[0] = part
-        for step, peer in enumerate(grp_peers):
-            ss_copies.append(pltpu.make_async_remote_copy(
-                src_ref=squares.at[0], dst_ref=squares.at[step + 1],
-                send_sem=ss_send.at[step], recv_sem=ss_recv.at[step],
-                device_id=at_grp(peer), device_id_type=MESH))
-            ss_copies[-1].start()
-
-    for chunk in range(first, chunk_n):
-        @pl.when(has_left)
-        def _():
-            u_copy(chunk).wait_recv()
-
-    lax.fori_loop(first * per_chunk, tile_n, halo_q, 0, unroll=UNROLL)
-    send_out(out_q, qg_hbm, top)
-
-    if whole_sum:
-        for copy in ss_copies:
-            copy.wait_recv()
-        ss = jnp.sum(jnp.sum(squares[...], axis=0), keepdims=True)
+        ss = jnp.sum(values * values, keepdims=True)
+        if far_peers:
+            ss = ss + jnp.sum(squares[...], keepdims=True)
         count = F32(raw.shape[0] * grp_n * LANES)
         factor = jnp.minimum(F32(1.0), jnp.sqrt(count / ss))
-        fg_ref[...] = gathered[...] * factor
+        fg_ref[...] = values * factor
         for copy in rs_copies + ag_copies + ss_copies:
             copy.wait_send()
 
@@ -323,6 +319,7 @@
     tile_n = chan // LANES
     chunk_n = 4 if tile_n % 4 == 0 else 1
     whole_sum = group_n % (8 * seq_n) == 0
+    far_n = max(1, (grp_n - 1) * seq_n)
     own = group_n // seq_n if whole_sum else 8
     dense = jax.ShapeDtypeStruct((rows, chan), BF16)
     anywhere = pl.BlockSpec(memory_space=pl.ANY)
@@ -332,9 +329,10 @@
     query_grad, key_grad, value_grad, sums = pl.pallas_call(
         functools.partial(kernel, seq_n, grp_n, whole_sum, chunk_n),
         out_shape=(dense, dense, dense, jax.ShapeDtypeStruct((group_n, tap_n), F32)),
-        in_specs=[anywhere] * 4 + [vmem],
+        in_specs=[anywhere] * 5,
         out_specs=(anywhere, anywhere, anywhere, vmem),
         scratch_shapes=[flat] * 4
+        + [pltpu.VMEM((group_n, tap_n), BF16)]
         + [pltpu.VMEM((tile_n, rows, LANES), BF16)] * 2
         + [pltpu.VMEM((tile_n, LANES, LANES), BF16)] * 2
         + [pltpu.VMEM((tile_n, PER_TILE * LANES, 2 * LANES), BF16)] * 2
@@ -344,10 +342,11 @@
             pltpu.VMEM((group_n, LANES), F32),
             pltpu.VMEM((seq_n, own, LANES), F32),
             pltpu.VMEM((group_n, LANES), F32),
-            pltpu.VMEM((grp_n, 8, LANES), F32),
-            dma((8,)), dma((6,)), dma((2, chunk_n)), dma((2, chunk_n)),
+            pltpu.VMEM((far_n, LANES), F32),
+            pltpu.VMEM((1, LANES), F32),
+            dma((9,)), dma((6,)), dma((2, chunk_n)), dma((2, chunk_n)),
             dma((seq_n,)), dma((seq_n,)), dma((seq_n,)), dma((seq_n,)),
-            dma((grp_n,)), dma((grp_n,)),
+            dma((far_n,)), dma((far_n,)),
         ],
         compiler_params=pltpu.CompilerParams(
             collective_id=0, has_side_effects=True, vmem_limit_bytes=60 * 1024 * 1024

time: 35.5 us -> 33.8 us (0.952)
  Pallas kernels: 30 us -> 28.4 us
    pallas_call x1, Pallas kernels: 30 us -> 28.4 us  [on_device(): pl.pallas_call(functools.partial(kernel, seq_n, grp_n, whole_sum, chunk_n...]
where the time goes in v3:
time: 33.8 us; the launch traced here: 33.6 us
  Pallas kernels  28.4 us (84%)
  local copies, waits for them, and re-layouts  4.57 us (14%)
  between operations  0.65 us (2%)
    pallas_call x1, Pallas kernels, on_device(): pl.pallas_call(functools.partial(kernel, seq_n, grp_n, whole_sum, chunk_n...  28.4 us
    unnamed x10, local copies, waits for them, and re-layouts  4.57 us

profile of v3, /device:TPU:0, one launch (start us, length us, event | category | flops | bytes accessed | tf_op | source)
XLA Modules:
  0.0 33.6 jit_solution(1032036337429366051)
XLA Ops:
  0.6 28.4 %shard_map.84 = (bf16[256,1024]{1,0:T(8,128)(2,1)}, bf16[256,1024]{1,0:T(8,128)(2,1)}, bf16[256,1024]{1,0:T(8,128)(2,1)}, f32[64,128]{1,0:T(8,128)}) custom-call(bf16[256,1024]{1,0:T(8,128)(2,1)} %q_hbm.1, bf16[256,1024]{1,0:T(8,128)(2,1)} %k_hbm.1, bf16[256,1024]{1,0:T(8,128)(2,1)} %v_hbm.1, bf16[256,1024]{1,0:T(8,128)(2,1)} %g_hbm.1, bf16[64,128]{1,0:T(8,128)(2,1)} %h_hbm.1), custom_call_target="tpu_custom_call" | custom-call | flops 3221225472 | bytes 3670016 | tf_op jit(solution)/shard_map/pallas_call | solution.py:329
  29.0 0.0 copy-start.1
  29.0 1.9 %copy.13 = bf16[256,1024]{1,0:T(8,128)(2,1)} copy(bf16[256,1024]{1,0:T(8,128)(2,1)} %get-tuple-element.8) | data formatting | bytes 1048576
  31.0 0.0 copy-done.1
  31.0 0.0 copy-start
  31.0 0.8 %copy.14 = bf16[256,1024]{1,0:T(8,128)(2,1)} copy(bf16[256,1024]{1,0:T(8,128)(2,1)S(1)} %copy-done.1) | data formatting | bytes 1048576
  31.8 0.4 %copy-done = bf16[256,1024]{1,0:T(8,128)(2,1)S(1)} copy-done((bf16[256,1024]{1,0:T(8,128)(2,1)S(1)}, bf16[256,1024]{1,0:T(8,128)(2,1)}, u32[]{:S(2)}) %copy-start) | copy-done | bytes 524312
  32.2 0.0 copy-start.2
  32.2 0.8 %copy.15 = bf16[256,1024]{1,0:T(8,128)(2,1)} copy(bf16[256,1024]{1,0:T(8,128)(2,1)S(1)} %copy-done) | data formatting | bytes 1048576
  33.0 0.0 copy-done.2
  33.0 0.6 %copy.16 = f32[64,128]{1,0:T(8,128)} copy(f32[64,128]{1,0:T(8,128)S(1)} %copy-done.2) | data formatting | bytes 65536
Async XLA Ops:
  29.0 1.9 %copy-start.1 = (bf16[256,1024]{1,0:T(8,128)(2,1)S(1)}, bf16[256,1024]{1,0:T(8,128)(2,1)}, u32[]{:S(2)}) copy-start(bf16[256,1024]{1,0:T(8,128)(2,1)} %get-tuple-element.9) | copy-start | bytes 1572868
  31.0 1.2 %copy-start = (bf16[256,1024]{1,0:T(8,128)(2,1)S(1)}, bf16[256,1024]{1,0:T(8,128)(2,1)}, u32[]{:S(2)}) copy-start(bf16[256,1024]{1,0:T(8,128)(2,1)} %get-tuple-element.10) | copy-start | bytes 1572868
  32.2 0.8 %copy-start.2 = (f32[64,128]{1,0:T(8,128)S(1)}, f32[64,128]{1,0:T(8,128)}, u32[]{:S(2)}) copy-start(f32[64,128]{1,0:T(8,128)} %get-tuple-element.11) | copy-start | bytes 98308
